TPU v7x, 256 devices: a whole 4x4x8 slice. The times are simulated.
256 devices in a mesh: mom: 16 (over z_hi, y, core), hist: 16 (over z_lo, x).
Axes of the slice: x: 4, y: 4, z: 8 (z_hi: 2, z_lo: 4; z = z_hi * 4 + z_lo), core: 2. Of those that a mesh axis runs over, the one named last changes fastest.
Arguments:
- green_row: float32 [6144, 256, 128], P('hist', 'mom'), may hold values from -6 to 6
- green_col: float32 [6144, 256, 128], P('hist', 'mom'), may hold values from -6 to 6
- screen: float32 [6144, 256, 128], P(('hist', 'mom')), may hold values from -2.5 to 2.5
- filled: int32 [16], P('hist'), may hold values from 1 to 384, 4608 in all
- sigma_mix: float32 [400, 256, 128], P('hist', 'mom'), may hold values from -6 to 6
- green_mix: float32 [400, 256, 128], P('hist', 'mom'), may hold values from -6 to 6
- green_now: float32 [256, 128], P('mom'), may hold values from -6 to 6
- hamilton: float32 [256, 128], P('mom'), may hold values from -2 to 2
Outputs:
- collision: float32 [256, 128], P('mom')
- green_next: float32 [256, 128], P('mom')
Inputs may be any that keep to these rules, and one draw needn't show every extreme that they name: filled[h] counts the used past-time slots of history group h, which are its first ones; the counts sum to 4608.
All inputs are finite; a program needn't handle non-finite values.
Results may differ from a plain program's by a relative error of at most 0.0003.
Values sent between devices are 32-bit elements; how exact they have to be, the bound alone decides.
No kernel may reach another device: no remote copies, remote signals or barrier semaphores. Data moves between devices by JAX's collectives and lax.ppermute only.
A program may use at most 128 MiB of HBM per device.

v0:
```python
import functools
import math

import jax
import jax.numpy as jnp
import numpy as np
from jax import lax
from jax.experimental import pallas as pl
from jax.experimental.pallas import tpu as pltpu
from jax.sharding import PartitionSpec as P

LAT = 16
ORBITAL_COUNT = 8
HALF = ORBITAL_COUNT * ORBITAL_COUNT
ROW = 2 * HALF
MEMORY_WEIGHT = 0.01
MIX_WEIGHT = 0.01
TIME_STEP = 0.1
HIGHEST = lax.Precision.HIGHEST
VMEM_LIMIT = 40 * 1024 * 1024


def split(values):
    high = values.astype(jnp.bfloat16)
    return high, (values - high.astype(jnp.float32)).astype(jnp.bfloat16)


def lattice_tables():
    points = np.arange(LAT)
    kx, ky = np.repeat(points, LAT), np.tile(points, LAT)
    phase = (kx[:, None] * kx[None, :] + ky[:, None] * ky[None, :]) % LAT
    angle = phase * (2.0 * math.pi / LAT)
    table = np.concatenate([np.cos(angle), np.sin(angle)]).astype(np.float32)
    high = table.astype(jnp.bfloat16)
    return high, (table - high.astype(np.float32)).astype(jnp.bfloat16)


def dot(first, second):
    return lax.dot_general(first, second, (((1,), (0,)), ((), ())), preferred_element_type=jnp.float32)


def times_i(values, low):
    turned = pltpu.roll(values, HALF, 1)
    return jnp.where(low, -turned, turned)


def sigma_kernel(high_ref, low_ref, green_ref, screen_ref, out_ref):
    points = LAT * LAT
    slots = screen_ref.shape[0]
    lane = lax.broadcasted_iota(jnp.int32, (points, ROW), 1)
    first = lane < HALF

    def turn(pair, sign):
        parts = [split(p) for p in pair]
        high = jnp.concatenate([p[0] for p in parts], axis=1)
        low = jnp.concatenate([p[1] for p in parts], axis=1)
        both = dot(high_ref[...], high) + (dot(high_ref[...], low) + dot(low_ref[...], high))
        out = []
        for i in range(len(pair)):
            here = both[:, i * ROW : (i + 1) * ROW]
            out.append(here[:points] + sign * times_i(here[points:], first))
        return out

    for s in range(0, slots, 2):
        space = turn([green_ref[:, s + i].reshape(points, ROW) for i in range(2)], 1.0)
        product = []
        for i in range(2):
            w = screen_ref[s + i] * (1.0 / points)
            w_turned = pltpu.roll(w, HALF, 1)
            g = space[i]
            g_turned = pltpu.roll(g, HALF, 1)
            product.append(g_turned * jnp.where(first, -w, w_turned) - g * jnp.where(first, w_turned, w))
        sigma = turn(product, -1.0)
        for i in range(2):
            out_ref[:, :, s + i, :] = sigma[i].reshape(LAT, LAT, ROW)


def sigma_of(green, screen):
    slots = screen.shape[0]
    step = 8
    high, low = lattice_tables()
    points = LAT * LAT
    return pl.pallas_call(
        sigma_kernel,
        grid=(slots // step,),
        in_specs=[
            pl.BlockSpec((2 * points, points), lambda i: (0, 0)),
            pl.BlockSpec((2 * points, points), lambda i: (0, 0)),
            pl.BlockSpec((LAT, step, LAT, ROW), lambda i: (0, i, 0, 0)),
            pl.BlockSpec((step, points, ROW), lambda i: (i, 0, 0)),
        ],
        out_specs=pl.BlockSpec((LAT, LAT, step, ROW), lambda i: (0, 0, i, 0)),
        out_shape=jax.ShapeDtypeStruct((LAT, LAT, slots, ROW), jnp.float32),
        compiler_params=pltpu.CompilerParams(vmem_limit_bytes=VMEM_LIMIT),
        cost_estimate=pl.CostEstimate(flops=slots * 12 * points * points * ROW, bytes_accessed=3 * slots * points * ROW * 4, transcendentals=0),
        name="sigma",
    )(jnp.asarray(high), jnp.asarray(low), green, screen)


def history_kernel(high_ref, low_ref, sigma_ref, spread_ref, mixed_ref, out_ref):
    owners, _, slots, _ = sigma_ref.shape
    lane = lax.broadcasted_iota(jnp.int32, (ORBITAL_COUNT, ROW), 1)
    sub = lax.broadcasted_iota(jnp.int32, (ORBITAL_COUNT, ROW), 0)
    inner = lane % ORBITAL_COUNT
    blocks = []
    for k in range(LAT):
        rows = sigma_ref[:, k].reshape(owners * slots, ROW)
        s_high, s_low = split(rows)
        c_high, c_low = high_ref[k], low_ref[k]
        outer = dot(c_high, s_high) + (dot(c_high, s_low) + dot(c_low, s_high))
        outer = outer.reshape(2, ORBITAL_COUNT, ORBITAL_COUNT, ROW)
        for part in range(2):
            picked = jnp.zeros((ORBITAL_COUNT, ROW), jnp.float32)
            for b in range(ORBITAL_COUNT):
                picked = jnp.where(inner == b, outer[part, b], picked)
            blocks.append(picked)
    picked = jnp.concatenate(blocks, axis=0)
    p_high, p_rest = split(picked)
    p_low = p_rest
    spread = spread_ref[...]
    summed = dot(p_high, spread) + dot(p_low, spread)
    summed = summed.reshape(2 * LAT, ORBITAL_COUNT, ROW)
    summed = jnp.sum(jnp.where((inner == sub)[None], summed, 0.0), axis=1).reshape(LAT, 2, ROW)
    low_half = lax.broadcasted_iota(jnp.int32, (LAT, ROW), 1) < HALF
    out_ref[...] = MEMORY_WEIGHT * (summed[:, 0] + times_i(summed[:, 1], low_half)) + mixed_ref[...]


def spread_table():
    group = np.arange(ROW) // ORBITAL_COUNT
    return (group[:, None] == group[None, :]).astype(jnp.bfloat16)


def history_of(high, low, sigma, mixed):
    return pl.pallas_call(
        history_kernel,
        out_shape=jax.ShapeDtypeStruct((LAT, ROW), jnp.float32),
        compiler_params=pltpu.CompilerParams(vmem_limit_bytes=VMEM_LIMIT),
        cost_estimate=pl.CostEstimate(flops=16 * 6 * 384 * ROW * ROW, bytes_accessed=2 * 384 * 16 * ROW * 4, transcendentals=0),
        name="history",
    )(high, low, sigma, jnp.asarray(spread_table()), mixed)


def complex_product(left, right):
    def contract(first, second):
        return jnp.einsum("kab,kbc->kac", first, second, precision=HIGHEST)

    return (
        contract(left[:, 0], right[:, 0]) - contract(left[:, 1], right[:, 1]),
        contract(left[:, 0], right[:, 1]) + contract(left[:, 1], right[:, 0]),
    )


def free_step(green_now, hamilton):
    shape = (green_now.shape[0], 2, ORBITAL_COUNT, ORBITAL_COUNT)
    green, ham = green_now.reshape(shape), hamilton.reshape(shape)
    left_re, left_im = complex_product(ham, green)
    right_re, right_im = complex_product(green, ham)
    moved = jnp.stack([left_im - right_im, right_re - left_re], axis=1)
    return green_now + TIME_STEP * moved.reshape(green_now.shape)


def mixed_sum(sigma_mix, green_mix):
    taus, points, _ = sigma_mix.shape
    left = sigma_mix.reshape(taus, points, 2, ORBITAL_COUNT, ORBITAL_COUNT)
    right = green_mix.reshape(taus, points, 2, ORBITAL_COUNT, ORBITAL_COUNT)

    def contract(first, second):
        return jnp.einsum("skab,skbc->kac", first, second, precision=HIGHEST).reshape(points, HALF)

    real = contract(left[:, :, 0], right[:, :, 0]) - contract(left[:, :, 1], right[:, :, 1])
    imag = contract(left[:, :, 0], right[:, :, 1]) + contract(left[:, :, 1], right[:, :, 0])
    return MIX_WEIGHT * jnp.concatenate([imag, -real], axis=-1)


def finish_kernel(parts_ref, free_ref, adjoint_ref, collision_ref, next_ref):
    collision = parts_ref[0]
    for i in range(1, parts_ref.shape[0]):
        collision = collision + parts_ref[i]
    high, rest = split(collision)
    middle, low = split(collision - high.astype(jnp.float32))
    adjoint = adjoint_ref[...]
    turned = dot(high, adjoint) + (dot(middle, adjoint) + dot(low, adjoint))
    collision_ref[...] = collision
    next_ref[...] = free_ref[...] - TIME_STEP * (collision + turned)


def adjoint_table():
    table = np.zeros((ROW, ROW), np.float32)
    for a in range(ORBITAL_COUNT):
        for c in range(ORBITAL_COUNT):
            table[a * ORBITAL_COUNT + c, c * ORBITAL_COUNT + a] = 1.0
            table[HALF + a * ORBITAL_COUNT + c, HALF + c * ORBITAL_COUNT + a] = -1.0
    return table.astype(jnp.bfloat16)


def finish(parts, free):
    out = jax.ShapeDtypeStruct(free.shape, jnp.float32)
    return pl.pallas_call(finish_kernel, out_shape=(out, out), name="finish")(parts, free, jnp.asarray(adjoint_table()))


def per_device(green_row, green_col, screen, filled, sigma_mix, green_mix, green_now, hamilton):
    slot_count, local_k, _ = green_row.shape
    owners = lax.axis_size("mom")
    own = slot_count // owners
    moved = lax.all_to_all(green_row.reshape(owners, own, local_k, ROW), "mom", 0, 0)
    sigma = sigma_of(moved, screen)
    arrived = lax.all_to_all(sigma, "mom", 0, 0)

    valid = jnp.arange(slot_count, dtype=jnp.int32) < filled[0]
    column = jnp.where(valid[:, None, None], green_col, 0.0)
    column = jnp.transpose(column, (1, 2, 0))
    high = lax.reduce_precision(column, 8, 7)
    high, low = high.astype(jnp.bfloat16), (column - high).astype(jnp.bfloat16)
    partial_sum = history_of(high, low, arrived, mixed_sum(sigma_mix, green_mix))
    groups = lax.axis_size("hist")
    parts = lax.all_to_all(jnp.broadcast_to(partial_sum[None], (groups, local_k, ROW)), "hist", 0, 0)
    return finish(parts, free_step(green_now, hamilton))


def solution(mesh):
    return jax.shard_map(
        per_device,
        mesh=mesh,
        in_specs=(
            P("hist", "mom", None),
            P("hist", "mom", None),
            P(("hist", "mom"), None, None),
            P("hist"),
            P("hist", "mom", None),
            P("hist", "mom", None),
            P("mom", None),
            P("mom", None),
        ),
        out_specs=(P("mom", None), P("mom", None)),
        check_vma=False,
    )
```

profile of v0, /device:TPU:24, one launch (start us, length us, event | category | flops | bytes accessed | tf_op | source)
XLA Modules:
  0.0 204.4 jit_solution(1956612581197829977)
XLA Ops:
  0.7 62.8 %all_to_all.15.green_ref = f32[16,24,16,128]{3,2,1,0:T(8,128)S(1)} all-to-all(f32[16,24,16,128]{3,2,1,0:T(8,128)} %bitcast.96), channel_id=1, replica_groups=mesh['mom'=16,'hist'=16] {'mom'}, dimensions={0} | all-to-all | bytes 6291456 | tf_op jit(solution)/shard_map/all_to_all | solution.py:205
  63.5 9.7 %sigma.1 = f32[16,16,24,128]{3,2,1,0:T(8,128)} custom-call(bf16[512,256]{1,0:T(8,128)(2,1)S(1)} %copy-done.3, bf16[512,256]{1,0:T(8,128)(2,1)S(1)} %copy-done.4, f32[16,24,16,128]{3,2,1,0:T(8,128)S(1)} %all_to_all.15.green_ref, f32[24,256,128]{2,1,0:T(8,128)S(1)} %copy-done.2), custom_call_target="tpu_custom_call" | custom-call | flops 2415919104 | bytes 9437184 | tf_op jit(solution)/shard_map/sigma/pallas_call | solution.py:83
  73.1 28.4 %all-to-all-start.1 = ((f32[16,16,24,128]{3,2,1,0:T(8,128)}), f32[16,16,24,128]{3,2,1,0:T(8,128)S(1)}, u32[]{:S(2)}, u32[]{:S(2)}) async-start(f32[16,16,24,128]{3,2,1,0:T(8,128)} %sigma.1), calls=%async_computation.1 | async-start | bytes 6291456 | tf_op jit(solution)/shard_map/all_to_all | solution.py:207
  101.5 3.6 %copy.35 = f32[384,16,128]{0,2,1:T(8,128)} copy(f32[384,16,128]{2,1,0:T(8,128)} %param.13) | data formatting | bytes 6291456 | tf_op args[1]
  105.8 1.4 copy.36
  107.3 1.3 copy.38
  108.6 1.4 fusion.28
  110.0 0.9 copy-done.8
  110.9 2.2 %convolution_bitcast_fusion = f32[16,8,8]{2,1,0:T(8,128)S(1)} fusion(f32[25,16,1,8,8]{0,4,3,2,1:T(8,128)S(1)} %get-tuple-element.5, f32[25,16,2,8,8]{0,4,3,2,1:T(8,128)} %bitcast.91), kind=kOutput, calls=%fused_computation.3 | convolution fusion | flops 2457600 | bytes 630784 | tf_op jit(solution)/shard_map/skab,skbc->kac/dot_general | solution.py:168
  113.1 1.2 fusion.3
  114.4 2.3 %convolution_bitcast_fusion.2 = f32[16,8,8]{2,1,0:T(8,128)S(1)} fusion(f32[25,16,1,8,8]{0,4,3,2,1:T(8,128)} %copy-done.8, f32[25,16,2,8,8]{0,4,3,2,1:T(8,128)} %bitcast.92), kind=kOutput, calls=%fused_computation.5 | convolution fusion | flops 2457600 | bytes 1052672 | tf_op jit(solution)/shard_map/skab,skbc->kac/dot_general | solution.py:168
  116.7 2.2 %fusion.1 = f32[16,8,8]{2,1,0:T(8,128)S(1)} fusion(f32[16,8,8]{2,1,0:T(8,128)S(1)} %convolution_bitcast_fusion.2, f32[25,16,1,8,8]{0,4,3,2,1:T(8,128)} %copy-done.7, f32[25,16,2,8,8]{0,4,3,2,1:T(8,128)} %bitcast.93), kind=kOutput, calls=%fused_computation.7 | convolution fusion | flops 2458624 | bytes 1056768 | tf_op jit(solution)/shard_map/skab,skbc->kac/dot_general | solution.py:168
  119.0 0.7 copy.44
  120.1 0.3 fusion.4
  121.0 0.3 fusion.6
  121.2 0.7 copy.56
  122.2 0.7 copy.57
  123.2 0.7 copy.54
  124.1 0.7 copy.55
  125.2 0.3 fusion.10
  125.5 0.8 maximum_multiply_fusion.1.mixed_ref
  126.3 4.3 %fusion = (bf16[16,128,384]{2,1,0:T(8,128)(2,1)}, bf16[16,128,384]{2,1,0:T(8,128)(2,1)}) fusion(f32[384,16,128]{0,2,1:T(8,128)} %copy.35, pred[384]{0:T(512)(128)(4,1)S(1)} %iota_compare_fusion), kind=kLoop, calls=%fused_computation.2 | loop fusion | flops 3932160 | bytes 6291840 | tf_op jit(solution)/shard_map/convert_element_type | solution.py:213
  130.6 17.3 %all-to-all-done.1.sigma_ref = f32[16,16,24,128]{3,2,1,0:T(8,128)S(1)} async-done(((f32[16,16,24,128]{3,2,1,0:T(8,128)}), f32[16,16,24,128]{3,2,1,0:T(8,128)S(1)}, u32[]{:S(2)}, u32[]{:S(2)}) %all-to-all-start.1) | async-done | bytes 3145760 | tf_op jit(solution)/shard_map/all_to_all | solution.py:207
  147.9 1.4 copy-done
  149.3 1.4 copy-done.1
  150.7 1.7 history.1
  152.4 0.7 broadcast_in_dim.21
  153.1 40.0 %all-to-all-start.2 = ((f32[16,16,128]{2,1,0:T(8,128)}), f32[16,16,128]{2,1,0:T(8,128)S(1)}, u32[]{:S(2)}, u32[]{:S(2)}) async-start(f32[16,16,128]{2,1,0:T(8,128)} %broadcast_in_dim.21), calls=%async_computation.2 | async-start | bytes 262144 | tf_op jit(solution)/shard_map/all_to_all | solution.py:216
  193.2 0.6 add.19.free_ref
  193.9 8.2 %all-to-all-done.2.parts_ref = f32[16,16,128]{2,1,0:T(8,128)S(1)} async-done(((f32[16,16,128]{2,1,0:T(8,128)}), f32[16,16,128]{2,1,0:T(8,128)S(1)}, u32[]{:S(2)}, u32[]{:S(2)}) %all-to-all-start.2) | async-done | bytes 131104 | tf_op jit(solution)/shard_map/all_to_all | solution.py:216
  202.1 0.7 copy-done.9
  202.8 1.7 finish.1
  (56 shorter events, 2.5 us)
Async XLA Ops:
  0.6 62.8 %copy-start.2 = (f32[24,256,128]{2,1,0:T(8,128)S(1)}, f32[24,256,128]{2,1,0:T(8,128)}, u32[]{:S(2)}) copy-start(f32[24,256,128]{2,1,0:T(8,128)} %screen_ref.1) | copy-start | bytes 9437188
  0.6 62.8 %copy-start.3 = (bf16[512,256]{1,0:T(8,128)(2,1)S(1)}, bf16[512,256]{1,0:T(8,128)(2,1)}, u32[]{:S(2)}) copy-start(bf16[512,256]{1,0:T(8,128)(2,1)} %constant.14.clone.high_ref) | copy-start | bytes 786436
  0.7 62.8 %copy-start.4 = (bf16[512,256]{1,0:T(8,128)(2,1)S(1)}, bf16[512,256]{1,0:T(8,128)(2,1)}, u32[]{:S(2)}) copy-start(bf16[512,256]{1,0:T(8,128)(2,1)} %constant.15.clone.low_ref) | copy-start | bytes 786436
  73.1 74.7 %all-to-all-start.1 = ((f32[16,16,24,128]{3,2,1,0:T(8,128)}), f32[16,16,24,128]{3,2,1,0:T(8,128)S(1)}, u32[]{:S(2)}, u32[]{:S(2)}) async-start(f32[16,16,24,128]{3,2,1,0:T(8,128)} %sigma.1), calls=%async_computation.1 | async-start | bytes 6291456 | tf_op jit(solution)/shard_map/all_to_all | solution.py:207
  101.5 4.3 %copy-start.10 = (f32[25,16,128]{2,1,0:T(8,128)S(1)}, f32[25,16,128]{2,1,0:T(8,128)}, u32[]{:S(2)}) copy-start(f32[25,16,128]{2,1,0:T(8,128)} %param.16) | copy-start | bytes 614404
  101.5 5.8 %copy-start.11 = (f32[25,16,128]{2,1,0:T(8,128)S(1)}, f32[25,16,128]{2,1,0:T(8,128)}, u32[]{:S(2)}) copy-start(f32[25,16,128]{2,1,0:T(8,128)} %param.17) | copy-start | bytes 614404
  108.6 4.4 %copy-start.6 = (f32[25,16,128]{0,2,1:T(8,128)S(1)}, f32[25,16,128]{0,2,1:T(8,128)}, u32[]{:S(2)}) copy-start(f32[25,16,128]{0,2,1:T(8,128)} %copy.38) | copy-start | bytes 614404
  108.6 11.1 %copy-start.16 = (f32[16,128]{1,0:T(8,128)S(1)}, f32[16,128]{1,0:T(8,128)}, u32[]{:S(2)}) copy-start(f32[16,128]{1,0:T(8,128)} %param.18) | copy-start | bytes 24580
  108.6 11.3 %copy-start.17 = (f32[16,128]{1,0:T(8,128)S(1)}, f32[16,128]{1,0:T(8,128)}, u32[]{:S(2)}) copy-start(f32[16,128]{1,0:T(8,128)} %param.19) | copy-start | bytes 24580
  110.0 0.9 copy-start.8
  110.0 3.0 %copy-start.7 = (f32[25,16,1,8,8]{0,4,3,2,1:T(8,128)}, f32[25,16,1,8,8]{0,4,3,2,1:T(8,128)S(1)}, u32[]{:S(2)}) copy-start(f32[25,16,1,8,8]{0,4,3,2,1:T(8,128)S(1)} %get-tuple-element.4) | copy-start | bytes 307204
  126.3 21.6 %copy-start.5 = (bf16[128,128]{1,0:T(8,128)(2,1)S(1)}, bf16[128,128]{1,0:T(8,128)(2,1)}, u32[]{:S(2)}) copy-start(bf16[128,128]{1,0:T(8,128)(2,1)} %constant.16.clone.spread_ref) | copy-start | bytes 98308
  147.9 1.4 copy-start
  149.3 1.4 copy-start.1
  150.7 42.4 %copy-start.12 = (f32[16,8,8]{0,2,1:T(8,128)S(1)}, f32[16,8,8]{0,2,1:T(8,128)}, u32[]{:S(2)}) copy-start(f32[16,8,8]{0,2,1:T(8,128)} %copy.56) | copy-start | bytes 12292
  150.7 42.4 %copy-start.13 = (f32[16,8,8]{0,2,1:T(8,128)S(1)}, f32[16,8,8]{0,2,1:T(8,128)}, u32[]{:S(2)}) copy-start(f32[16,8,8]{0,2,1:T(8,128)} %copy.57) | copy-start | bytes 12292
  150.7 42.4 %copy-start.14 = (f32[16,8,8]{0,2,1:T(8,128)S(1)}, f32[16,8,8]{0,2,1:T(8,128)}, u32[]{:S(2)}) copy-start(f32[16,8,8]{0,2,1:T(8,128)} %copy.54) | copy-start | bytes 12292
  150.7 42.4 %copy-start.15 = (f32[16,8,8]{0,2,1:T(8,128)S(1)}, f32[16,8,8]{0,2,1:T(8,128)}, u32[]{:S(2)}) copy-start(f32[16,8,8]{0,2,1:T(8,128)} %copy.55) | copy-start | bytes 12292
  153.1 49.0 %all-to-all-start.2 = ((f32[16,16,128]{2,1,0:T(8,128)}), f32[16,16,128]{2,1,0:T(8,128)S(1)}, u32[]{:S(2)}, u32[]{:S(2)}) async-start(f32[16,16,128]{2,1,0:T(8,128)} %broadcast_in_dim.21), calls=%async_computation.2 | async-start | bytes 262144 | tf_op jit(solution)/shard_map/all_to_all | solution.py:216
  202.1 0.7 copy-start.9
where the time goes:
time: 205 us; the launch traced here: 204 us
  starting transfers between devices  68.4 us (33%)
  blocking collectives  62.8 us (31%)
  waiting for transfers between devices  25.5 us (12%)
  local copies, waits for them, and re-layouts  17.5 us (9%)
  Pallas kernels  13.1 us (6%)
  matrix products  9.87 us (5%)
  other arithmetic  5.71 us (3%)
    all_to_all x1, blocking collectives, per_device(): lax.all_to_all(green_row.reshape(owners, own, local_k, ROW), 'mom', 0, 0)  62.8 us
    all_to_all x1, starting transfers between devices, per_device(): lax.all_to_all(jnp.broadcast_to(partial_sum[None], (groups, local_k, ROW)...  40 us
    all_to_all x1, starting transfers between devices, per_device(): arrived = lax.all_to_all(sigma, 'mom', 0, 0)  28.4 us
    all_to_all x1, waiting for transfers between devices, per_device(): arrived = lax.all_to_all(sigma, 'mom', 0, 0)  17.3 us
    unnamed x45, local copies, waits for them, and re-layouts  11.3 us
    pallas_call x1, Pallas kernels, sigma_of(): pl.pallas_call(sigma_kernel, grid=(slots // step,), in_specs=[pl.BlockSpe...  9.66 us
    all_to_all x1, waiting for transfers between devices, per_device(): lax.all_to_all(jnp.broadcast_to(partial_sum[None], (groups, local_k, ROW)...  8.25 us
    dot_general x4, matrix products, contract(): jnp.einsum('skab,skbc->kac', first, second, precision=HIGHEST)  7.86 us
  transfers between devices with their start and end apart: 2, of which 2 were waited for; matrix products, arithmetic and copies ran while one was open for 14% of the time, Pallas kernels for 0%

commit v1 on v0

--- a/solution.py
+++ b/solution.py
@@ -17,7 +17,8 @@
 MIX_WEIGHT = 0.01
 TIME_STEP = 0.1
 HIGHEST = lax.Precision.HIGHEST
-VMEM_LIMIT = 40 * 1024 * 1024
+RUN = 4
+VMEM_LIMIT = 20 * 1024 * 1024
 
 
 def split(values):
@@ -26,13 +27,19 @@
 
 
 def lattice_tables():
-    points = np.arange(LAT)
-    kx, ky = np.repeat(points, LAT), np.tile(points, LAT)
-    phase = (kx[:, None] * kx[None, :] + ky[:, None] * ky[None, :]) % LAT
-    angle = phase * (2.0 * math.pi / LAT)
-    table = np.concatenate([np.cos(angle), np.sin(angle)]).astype(np.float32)
-    high = table.astype(jnp.bfloat16)
-    return high, (table - high.astype(np.float32)).astype(jnp.bfloat16)
+    points, half = np.arange(LAT), np.arange(LAT // 2)
+    kx, ky = np.repeat(half, LAT), np.tile(points, LAT // 2)
+    tables = []
+    for odd in range(2):
+        rx, ry = np.repeat(2 * half + odd, LAT), np.tile(points, LAT // 2)
+        angle = (rx[:, None] * kx[None, :] + ry[:, None] * ky[None, :]) % LAT * (2.0 * math.pi / LAT)
+        tables.append([np.concatenate([np.cos(a), np.sin(a)]) for a in (angle, angle.T)])
+    out = []
+    for table in (np.stack([t[0] for t in tables]), np.stack([t[1] for t in tables])):
+        table = table.astype(np.float32)
+        high = table.astype(jnp.bfloat16)
+        out += [np.concatenate([high, high], axis=2), (table - high.astype(np.float32)).astype(jnp.bfloat16)]
+    return out
 
 
 def dot(first, second):
@@ -44,57 +51,55 @@
     return jnp.where(low, -turned, turned)
 
 
-def sigma_kernel(high_ref, low_ref, green_ref, screen_ref, out_ref):
+def sigma_kernel(to_space_ref, to_space_low_ref, back_ref, back_low_ref, green_ref, screen_ref, out_ref):
     points = LAT * LAT
+    half = points // 2
     slots = screen_ref.shape[0]
-    lane = lax.broadcasted_iota(jnp.int32, (points, ROW), 1)
-    first = lane < HALF
-
-    def turn(pair, sign):
-        parts = [split(p) for p in pair]
-        high = jnp.concatenate([p[0] for p in parts], axis=1)
-        low = jnp.concatenate([p[1] for p in parts], axis=1)
-        both = dot(high_ref[...], high) + (dot(high_ref[...], low) + dot(low_ref[...], high))
+    first = lax.broadcasted_iota(jnp.int32, (half, ROW), 1) < HALF
+
+    def turn(values, table, table_low, sign):
+        high, low = split(values)
+        both = dot(table, jnp.concatenate([high, low], axis=0)) + dot(table_low, high)
         out = []
-        for i in range(len(pair)):
+        for i in range(2):
             here = both[:, i * ROW : (i + 1) * ROW]
-            out.append(here[:points] + sign * times_i(here[points:], first))
+            out.append(here[:half] + sign * times_i(here[half:], first))
         return out
 
+    done = []
     for s in range(0, slots, 2):
-        space = turn([green_ref[:, s + i].reshape(points, ROW) for i in range(2)], 1.0)
-        product = []
+        lower = jnp.concatenate([green_ref[: LAT // 2, s + i].reshape(half, ROW) for i in range(2)], axis=1)
+        upper = jnp.concatenate([green_ref[LAT // 2 :, s + i].reshape(half, ROW) for i in range(2)], axis=1)
+        turned = []
+        for odd in range(2):
+            space = turn(lower - upper if odd else lower + upper, to_space_ref[odd], to_space_low_ref[odd], 1.0)
+            product = []
+            for i in range(2):
+                w = screen_ref[s + i].reshape(LAT // 2, 2, LAT, ROW)[:, odd].reshape(half, ROW) * (1.0 / points)
+                w_turned = pltpu.roll(w, HALF, 1)
+                g = space[i]
+                g_turned = pltpu.roll(g, HALF, 1)
+                product.append(g_turned * jnp.where(first, -w, w_turned) - g * jnp.where(first, w_turned, w))
+            turned.append(turn(jnp.concatenate(product, axis=1), back_ref[odd], back_low_ref[odd], -1.0))
         for i in range(2):
-            w = screen_ref[s + i] * (1.0 / points)
-            w_turned = pltpu.roll(w, HALF, 1)
-            g = space[i]
-            g_turned = pltpu.roll(g, HALF, 1)
-            product.append(g_turned * jnp.where(first, -w, w_turned) - g * jnp.where(first, w_turned, w))
-        sigma = turn(product, -1.0)
-        for i in range(2):
-            out_ref[:, :, s + i, :] = sigma[i].reshape(LAT, LAT, ROW)
+            even, odd = turned[0][i], turned[1][i]
+            done.append(jnp.concatenate([even + odd, even - odd], axis=0))
+        if len(done) == 8:
+            block = jnp.swapaxes(jnp.stack(done), 0, 1)
+            out_ref[:, :, s - 6 : s + 2, :] = block.reshape(LAT, LAT, 8, ROW)
+            done = []
 
 
 def sigma_of(green, screen):
     slots = screen.shape[0]
-    step = 8
-    high, low = lattice_tables()
     points = LAT * LAT
     return pl.pallas_call(
         sigma_kernel,
-        grid=(slots // step,),
-        in_specs=[
-            pl.BlockSpec((2 * points, points), lambda i: (0, 0)),
-            pl.BlockSpec((2 * points, points), lambda i: (0, 0)),
-            pl.BlockSpec((LAT, step, LAT, ROW), lambda i: (0, i, 0, 0)),
-            pl.BlockSpec((step, points, ROW), lambda i: (i, 0, 0)),
-        ],
-        out_specs=pl.BlockSpec((LAT, LAT, step, ROW), lambda i: (0, 0, i, 0)),
         out_shape=jax.ShapeDtypeStruct((LAT, LAT, slots, ROW), jnp.float32),
         compiler_params=pltpu.CompilerParams(vmem_limit_bytes=VMEM_LIMIT),
-        cost_estimate=pl.CostEstimate(flops=slots * 12 * points * points * ROW, bytes_accessed=3 * slots * points * ROW * 4, transcendentals=0),
+        cost_estimate=pl.CostEstimate(flops=slots * 8 * points * points * ROW, bytes_accessed=3 * slots * points * ROW * 4, transcendentals=0),
         name="sigma",
-    )(jnp.asarray(high), jnp.asarray(low), green, screen)
+    )(*map(jnp.asarray, lattice_tables()), green, screen)
 
 
 def history_kernel(high_ref, low_ref, sigma_ref, spread_ref, mixed_ref, out_ref):
@@ -122,7 +127,8 @@
     summed = summed.reshape(2 * LAT, ORBITAL_COUNT, ROW)
     summed = jnp.sum(jnp.where((inner == sub)[None], summed, 0.0), axis=1).reshape(LAT, 2, ROW)
     low_half = lax.broadcasted_iota(jnp.int32, (LAT, ROW), 1) < HALF
-    out_ref[...] = MEMORY_WEIGHT * (summed[:, 0] + times_i(summed[:, 1], low_half)) + mixed_ref[...]
+    total = MEMORY_WEIGHT * (summed[:, 0] + times_i(summed[:, 1], low_half)) + mixed_ref[...]
+    out_ref[...] = jnp.broadcast_to(total[None], out_ref.shape)
 
 
 def spread_table():
@@ -130,10 +136,10 @@
     return (group[:, None] == group[None, :]).astype(jnp.bfloat16)
 
 
-def history_of(high, low, sigma, mixed):
+def history_of(high, low, sigma, mixed, copies):
     return pl.pallas_call(
         history_kernel,
-        out_shape=jax.ShapeDtypeStruct((LAT, ROW), jnp.float32),
+        out_shape=jax.ShapeDtypeStruct((copies, LAT, ROW), jnp.float32),
         compiler_params=pltpu.CompilerParams(vmem_limit_bytes=VMEM_LIMIT),
         cost_estimate=pl.CostEstimate(flops=16 * 6 * 384 * ROW * ROW, bytes_accessed=2 * 384 * 16 * ROW * 4, transcendentals=0),
         name="history",
@@ -202,19 +208,30 @@
     slot_count, local_k, _ = green_row.shape
     owners = lax.axis_size("mom")
     own = slot_count // owners
+    run = lax.axis_index("hist") // RUN
+    early = (run + 1) // 2 % 2 == 1
+
+    def local_work():
+        return mixed_sum(sigma_mix, green_mix), free_step(green_now, hamilton)
+
+    def nothing():
+        return jax.tree.map(lambda leaf: jnp.zeros(leaf.shape, leaf.dtype), jax.eval_shape(local_work))
+
+    ready = lax.cond(early, nothing, local_work)
+    green_row, ready = lax.optimization_barrier((green_row, ready))
     moved = lax.all_to_all(green_row.reshape(owners, own, local_k, ROW), "mom", 0, 0)
     sigma = sigma_of(moved, screen)
     arrived = lax.all_to_all(sigma, "mom", 0, 0)
-
     valid = jnp.arange(slot_count, dtype=jnp.int32) < filled[0]
     column = jnp.where(valid[:, None, None], green_col, 0.0)
     column = jnp.transpose(column, (1, 2, 0))
     high = lax.reduce_precision(column, 8, 7)
     high, low = high.astype(jnp.bfloat16), (column - high).astype(jnp.bfloat16)
-    partial_sum = history_of(high, low, arrived, mixed_sum(sigma_mix, green_mix))
-    groups = lax.axis_size("hist")
-    parts = lax.all_to_all(jnp.broadcast_to(partial_sum[None], (groups, local_k, ROW)), "hist", 0, 0)
-    return finish(parts, free_step(green_now, hamilton))
+    ready, _ = lax.optimization_barrier((ready, moved))
+    mixed, free = lax.cond(early, local_work, lambda: ready)
+    partial_sums = history_of(high, low, arrived, mixed, lax.axis_size("hist"))
+    parts = lax.all_to_all(partial_sums, "hist", 0, 0)
+    return finish(parts, free)
 
 
 def solution(mesh):

time: 205 us -> 189 us (0.922)
  starting transfers between devices: 68.4 us -> 9.32 us
  waiting for transfers between devices: 25.5 us -> 54.3 us
  blocking collectives: 62.8 us -> 90.9 us
  local copies, waits for them, and re-layouts: 17.5 us -> 12.5 us
  Pallas kernels: 13.1 us -> 8.71 us
  matrix products: 9.87 us -> 6.53 us
    all_to_all x1 -> x0, starting transfers between devices: 40 us -> none  [per_device(): lax.all_to_all(jnp.broadcast_to(partial_sum[None], (groups, local_k, ROW)...]
    all_to_all x1, waiting for transfers between devices: 17.3 us -> 54.3 us  [per_device(): arrived = lax.all_to_all(sigma, 'mom', 0, 0)]
    all_to_all x1, starting transfers between devices: 28.4 us -> 9.32 us  [per_device(): arrived = lax.all_to_all(sigma, 'mom', 0, 0)]
    all_to_all x0 -> x1, blocking collectives: none -> 15.7 us  [per_device(): parts = lax.all_to_all(partial_sums, 'hist', 0, 0)]
    all_to_all x1, blocking collectives: 62.8 us -> 75.2 us  [per_device(): lax.all_to_all(green_row.reshape(owners, own, local_k, ROW), 'mom', 0, 0)]
    all_to_all x1 -> x0, waiting for transfers between devices: 8.25 us -> none  [per_device(): lax.all_to_all(jnp.broadcast_to(partial_sum[None], (groups, local_k, ROW)...]
    pallas_call x2, Pallas kernels: 11.4 us -> 7.03 us  [the longest x1 5.37 us: sigma_of(): pl.pallas_call(sigma_kernel, out_shape=jax.ShapeDtypeStruct((LAT, LAT, sl...]
    dot_general x4, matrix products: 7.86 us -> 4.5 us  [contract(): jnp.einsum('skab,skbc->kac', first, second, precision=HIGHEST)]
  transfers between devices with their start and end apart: 2 -> 1, of which waited for: 2 -> 1; matrix products, arithmetic and copies ran while one was open for 14% -> 5% of each run, Pallas kernels for 0% -> 0%
where the time goes in v1:
time: 189 us; the launch traced here: 188 us
  blocking collectives  90.9 us (48%)
  waiting for transfers between devices  54.3 us (29%)
  local copies, waits for them, and re-layouts  12.5 us (7%)
  starting transfers between devices  9.32 us (5%)
  Pallas kernels  8.71 us (5%)
  matrix products  6.53 us (3%)
  other arithmetic  4.37 us (2%)
    all_to_all x1, blocking collectives, per_device(): lax.all_to_all(green_row.reshape(owners, own, local_k, ROW), 'mom', 0, 0)  75.2 us
    all_to_all x1, waiting for transfers between devices, per_device(): arrived = lax.all_to_all(sigma, 'mom', 0, 0)  54.3 us
    all_to_all x1, blocking collectives, per_device(): parts = lax.all_to_all(partial_sums, 'hist', 0, 0)  15.7 us
    all_to_all x1, starting transfers between devices, per_device(): arrived = lax.all_to_all(sigma, 'mom', 0, 0)  9.32 us
    unnamed x23, local copies, waits for them, and re-layouts  8.09 us
    pallas_call x1, Pallas kernels, sigma_of(): pl.pallas_call(sigma_kernel, out_shape=jax.ShapeDtypeStruct((LAT, LAT, sl...  5.37 us
    dot_general x4, matrix products, contract(): jnp.einsum('skab,skbc->kac', first, second, precision=HIGHEST)  4.5 us
    convert_element_type x1, other arithmetic, per_device(): (column - high).astype(jnp.bfloat16)  4.24 us
  transfers between devices with their start and end apart: 1, of which 1 were waited for; matrix products, arithmetic and copies ran while one was open for 5% of the time, Pallas kernels for 0%

profile of v1, /device:TPU:24, one launch (start us, length us, event | category | flops | bytes accessed | tf_op | source)
XLA Modules:
  0.0 188.3 jit_solution(6798882986622526994)
XLA Ops:
  0.7 10.7 %conditional.2 = (f32[16,128]{1,0:T(8,128)S(1)}, f32[16,128]{0,1:T(8,128)S(1)}) conditional(s32[]{:T(128)} %convert_element_type.12, (f32[25,16,128]{2,1,0:T(8,128)}, f32[25,16,128]{2,1,0:T(8,128)}, f32[16,128]{1,0:T(8,128)}, f32[16,128]{1,0:T(8,128)}) %tuple.29, () %tuple.25), branch_computations={%region_0.1_spmd, %region_1.2_spmd} | conditional | flops 10636288 | bytes 7602248 | solution.py:220
  0.7 0.8 copy.132
  1.6 0.8 copy.131
  2.8 0.3 fusion.7
  3.1 0.3 fusion.5
  3.5 0.3 fusion.3
  3.8 0.3 fusion.9
  4.1 0.3 fusion.19
  4.5 0.3 fusion.21
  4.8 0.3 fusion.13
  5.1 0.3 fusion.11
  5.6 0.4 copy.130
  6.0 0.4 copy.129
  6.4 1.2 convolution_bitcast_fusion
  7.6 1.2 convolution_bitcast_fusion.2
  8.8 1.0 fusion
  9.8 1.2 fusion.2
  11.0 0.1 copy.91
  11.4 75.2 %all_to_all.15.green_ref = f32[16,24,16,128]{3,2,1,0:T(8,128)S(1)} all-to-all(f32[16,24,16,128]{3,2,1,0:T(8,128)} %bitcast.188), channel_id=1, replica_groups=mesh['mom'=16,'hist'=16] {'mom'}, dimensions={0} | all-to-all | bytes 6291456 | tf_op jit(solution)/shard_map/all_to_all | solution.py:222
  86.6 5.4 %sigma.1 = f32[16,16,24,128]{3,2,1,0:T(8,128)S(1)} custom-call(bf16[2,256,256]{2,1,0:T(8,128)(2,1)S(1)} %copy-done.5, bf16[2,256,128]{2,1,0:T(8,128)(2,1)S(1)} %copy-done.7, bf16[2,256,256]{2,1,0:T(8,128)(2,1)S(1)} %copy-done.4, bf16[2,256,128]{2,1,0:T(8,128)(2,1)S(1)} %copy-done.6, f32[16,24,16,128]{3,2,1,0:T(8,128)S(1)} %all_to_all.15.green_ref, ...), custom_call_target="tpu_custom_call" | custom-call | flops 1610612736 | bytes 9437184 | tf_op jit(solution)/shard_map/sigma/pallas_call | solution.py:96
  92.0 1.6 copy-done
  93.6 9.3 %all-to-all-start.1 = ((f32[16,16,24,128]{3,2,1,0:T(8,128)}), f32[16,16,24,128]{3,2,1,0:T(8,128)S(1)}, u32[]{:S(2)}, u32[]{:S(2)}) async-start(f32[16,16,24,128]{3,2,1,0:T(8,128)} %copy-done), calls=%async_computation.1 | async-start | bytes 6291456 | tf_op jit(solution)/shard_map/all_to_all | solution.py:224
  103.6 3.6 %copy.128 = f32[384,16,128]{0,2,1:T(8,128)} copy(f32[384,16,128]{2,1,0:T(8,128)} %param.19) | data formatting | bytes 6291456 | tf_op args[1]
  107.2 4.2 %fusion.54 = (bf16[16,128,384]{2,1,0:T(8,128)(2,1)}, bf16[16,128,384]{2,1,0:T(8,128)(2,1)}) fusion(f32[384,16,128]{0,2,1:T(8,128)} %copy.128, pred[384]{0:T(512)(128)(4,1)S(1)} %iota_compare_fusion), kind=kLoop, calls=%fused_computation.82 | loop fusion | flops 3932160 | bytes 6291840 | tf_op jit(solution)/shard_map/convert_element_type | solution.py:229
  111.5 0.7 conditional.3
  111.5 0.7 copy.146
  112.1 54.3 %all-to-all-done.1.sigma_ref = f32[16,16,24,128]{3,2,1,0:T(8,128)S(1)} async-done(((f32[16,16,24,128]{3,2,1,0:T(8,128)}), f32[16,16,24,128]{3,2,1,0:T(8,128)S(1)}, u32[]{:S(2)}, u32[]{:S(2)}) %all-to-all-start.1) | async-done | bytes 3145760 | tf_op jit(solution)/shard_map/all_to_all | solution.py:224
  166.4 1.4 copy-done.1
  167.8 1.4 copy-done.2
  169.3 1.7 history.1
  170.9 15.7 %all_to_all.16.parts_ref = f32[16,16,128]{2,1,0:T(8,128)} all-to-all(f32[16,16,128]{2,1,0:T(8,128)S(1)} %history.1), channel_id=1, replica_groups=mesh['mom'=16,'hist'=16] {'hist'}, dimensions={0} | all-to-all | bytes 262144 | tf_op jit(solution)/shard_map/all_to_all | solution.py:233
  186.6 1.7 finish.1
  (46 shorter events, 1.5 us)
Async XLA Ops:
  0.7 4.9 %copy-start.11 = (f32[25,16,128]{2,1,0:T(8,128)S(1)}, f32[25,16,128]{2,1,0:T(8,128)}, u32[]{:S(2)}) copy-start(f32[25,16,128]{2,1,0:T(8,128)} %get-tuple-element.69) | copy-start | bytes 614404 | tf_op jit(solution)/shard_map/cond
  0.7 5.3 %copy-start.10 = (f32[25,16,128]{2,1,0:T(8,128)S(1)}, f32[25,16,128]{2,1,0:T(8,128)}, u32[]{:S(2)}) copy-start(f32[25,16,128]{2,1,0:T(8,128)} %get-tuple-element.68) | copy-start | bytes 614404 | tf_op jit(solution)/shard_map/cond
  11.3 75.2 %copy-start.3 = (f32[24,256,128]{2,1,0:T(8,128)S(1)}, f32[24,256,128]{2,1,0:T(8,128)}, u32[]{:S(2)}) copy-start(f32[24,256,128]{2,1,0:T(8,128)} %screen_ref.1) | copy-start | bytes 9437188
  11.3 75.2 %copy-start.4 = (bf16[2,256,256]{2,1,0:T(8,128)(2,1)S(1)}, bf16[2,256,256]{2,1,0:T(8,128)(2,1)}, u32[]{:S(2)}) copy-start(bf16[2,256,256]{2,1,0:T(8,128)(2,1)} %constant.65.clone.back_ref) | copy-start | bytes 786436
  11.3 75.2 %copy-start.5 = (bf16[2,256,256]{2,1,0:T(8,128)(2,1)S(1)}, bf16[2,256,256]{2,1,0:T(8,128)(2,1)}, u32[]{:S(2)}) copy-start(bf16[2,256,256]{2,1,0:T(8,128)(2,1)} %constant.63.clone.to_space_ref) | copy-start | bytes 786436
  11.4 75.2 %copy-start.6 = (bf16[2,256,128]{2,1,0:T(8,128)(2,1)S(1)}, bf16[2,256,128]{2,1,0:T(8,128)(2,1)}, u32[]{:S(2)}) copy-start(bf16[2,256,128]{2,1,0:T(8,128)(2,1)} %constant.66.clone.back_low_ref) | copy-start | bytes 393220
  11.4 75.2 %copy-start.7 = (bf16[2,256,128]{2,1,0:T(8,128)(2,1)S(1)}, bf16[2,256,128]{2,1,0:T(8,128)(2,1)}, u32[]{:S(2)}) copy-start(bf16[2,256,128]{2,1,0:T(8,128)(2,1)} %constant.64.clone.to_space_low_ref) | copy-start | bytes 393220
  92.0 1.6 copy-start
  93.6 72.8 %all-to-all-start.1 = ((f32[16,16,24,128]{3,2,1,0:T(8,128)}), f32[16,16,24,128]{3,2,1,0:T(8,128)S(1)}, u32[]{:S(2)}, u32[]{:S(2)}) async-start(f32[16,16,24,128]{3,2,1,0:T(8,128)} %copy-done), calls=%async_computation.1 | async-start | bytes 6291456 | tf_op jit(solution)/shard_map/all_to_all | solution.py:224
  103.6 3.6 %copy-start.12 = (f32[16,128]{1,0:T(8,128)S(1)}, f32[16,128]{1,0:T(8,128)}, u32[]{:S(2)}) copy-start(f32[16,128]{1,0:T(8,128)} %param.25) | copy-start | bytes 24580
  103.6 3.6 %copy-start.13 = (f32[16,128]{1,0:T(8,128)S(1)}, f32[16,128]{1,0:T(8,128)}, u32[]{:S(2)}) copy-start(f32[16,128]{1,0:T(8,128)} %param.24) | copy-start | bytes 24580
  111.4 55.0 %copy-start.8 = (bf16[128,128]{1,0:T(8,128)(2,1)S(1)}, bf16[128,128]{1,0:T(8,128)(2,1)}, u32[]{:S(2)}) copy-start(bf16[128,128]{1,0:T(8,128)(2,1)} %constant.67.clone.spread_ref) | copy-start | bytes 98308
  166.4 1.4 copy-start.1
  167.8 1.4 copy-start.2

commit v2 on v1

--- a/solution.py
+++ b/solution.py
@@ -19,6 +19,20 @@
 HIGHEST = lax.Precision.HIGHEST
 RUN = 4
 VMEM_LIMIT = 20 * 1024 * 1024
+
+
+def exchange_order():
+    return np.arange(LAT).reshape(2, 4, 2).swapaxes(0, 1).reshape(LAT)
+
+
+def ordered(blocks):
+    rest = blocks.shape[1:]
+    return blocks.reshape(2, 4, 2, *rest).swapaxes(0, 1).reshape(LAT, *rest)
+
+
+def exchange(blocks):
+    groups = [[int(member) for member in exchange_order()]]
+    return lax.all_to_all(blocks, "mom", 0, 0, axis_index_groups=groups)
 
 
 def split(values):
@@ -66,6 +80,7 @@
             out.append(here[:half] + sign * times_i(here[half:], first))
         return out
 
+    spots = [int(spot) for spot in np.argsort(exchange_order())]
     done = []
     for s in range(0, slots, 2):
         lower = jnp.concatenate([green_ref[: LAT // 2, s + i].reshape(half, ROW) for i in range(2)], axis=1)
@@ -86,7 +101,9 @@
             done.append(jnp.concatenate([even + odd, even - odd], axis=0))
         if len(done) == 8:
             block = jnp.swapaxes(jnp.stack(done), 0, 1)
-            out_ref[:, :, s - 6 : s + 2, :] = block.reshape(LAT, LAT, 8, ROW)
+            block = block.reshape(LAT, LAT, 8, ROW)
+            for kx in range(LAT):
+                out_ref[spots[kx], :, s - 6 : s + 2, :] = block[kx]
             done = []
 
 
@@ -221,9 +238,10 @@
     green_row, ready = lax.optimization_barrier((green_row, ready))
     moved = lax.all_to_all(green_row.reshape(owners, own, local_k, ROW), "mom", 0, 0)
     sigma = sigma_of(moved, screen)
-    arrived = lax.all_to_all(sigma, "mom", 0, 0)
+    arrived = exchange(sigma)
     valid = jnp.arange(slot_count, dtype=jnp.int32) < filled[0]
     column = jnp.where(valid[:, None, None], green_col, 0.0)
+    column = ordered(column.reshape(owners, own, local_k, ROW)).reshape(slot_count, local_k, ROW)
     column = jnp.transpose(column, (1, 2, 0))
     high = lax.reduce_precision(column, 8, 7)
     high, low = high.astype(jnp.bfloat16), (column - high).astype(jnp.bfloat16)

time: 189 us -> 182 us (0.963)
  waiting for transfers between devices: 54.3 us -> 41.7 us
  other arithmetic: 4.37 us -> 7.67 us
  local copies, waits for them, and re-layouts: 12.5 us -> 14.6 us
    all_to_all x1, waiting for transfers between devices: 54.3 us -> 41.7 us  [exchange(): return lax.all_to_all(blocks, 'mom', 0, 0, axis_index_groups=groups)]
    another operation x4 -> x5, local copies, waits for them, and re-layouts: 2.36 us -> 5.97 us  [the longest x1 3.6 us: per_device(): ordered(column.reshape(owners, own, local_k, ROW))]
    unnamed x23 -> x24, local copies, waits for them, and re-layouts: 8.09 us -> 4.5 us
    select_n x0 -> x1, other arithmetic: none -> 2.69 us  [per_device(): column = jnp.where(valid[:, None, None], green_col, 0.0)]
    transpose x0 -> x1, local copies, waits for them, and re-layouts: none -> 2.02 us  [ordered(): return blocks.reshape(2, 4, 2, *rest).swapaxes(0, 1).reshape(LAT, *rest)]
  transfers between devices with their start and end apart: 1 -> 1, of which waited for: 1 -> 1; matrix products, arithmetic and copies ran while one was open for 5% -> 7% of each run, Pallas kernels for 0% -> 0%
where the time goes in v2:
time: 182 us; the launch traced here: 180 us
  blocking collectives  89.7 us (49%)
  waiting for transfers between devices  41.7 us (23%)
  local copies, waits for them, and re-layouts  14.6 us (8%)
  starting transfers between devices  9.33 us (5%)
  Pallas kernels  8.71 us (5%)
  other arithmetic  7.67 us (4%)
  matrix products  6.55 us (4%)
    all_to_all x1, blocking collectives, per_device(): lax.all_to_all(green_row.reshape(owners, own, local_k, ROW), 'mom', 0, 0)  75.1 us
    all_to_all x1, waiting for transfers between devices, exchange(): return lax.all_to_all(blocks, 'mom', 0, 0, axis_index_groups=groups)  41.7 us
    all_to_all x1, blocking collectives, per_device(): parts = lax.all_to_all(partial_sums, 'hist', 0, 0)  14.6 us
    all_to_all x1, starting transfers between devices, exchange(): return lax.all_to_all(blocks, 'mom', 0, 0, axis_index_groups=groups)  9.33 us
    pallas_call x1, Pallas kernels, sigma_of(): pl.pallas_call(sigma_kernel, out_shape=jax.ShapeDtypeStruct((LAT, LAT, sl...  5.37 us
    dot_general x4, matrix products, contract(): jnp.einsum('skab,skbc->kac', first, second, precision=HIGHEST)  4.52 us
    unnamed x24, local copies, waits for them, and re-layouts  4.5 us
    convert_element_type x1, other arithmetic, per_device(): (column - high).astype(jnp.bfloat16)  4.23 us
  transfers between devices with their start and end apart: 1, of which 1 were waited for; matrix products, arithmetic and copies ran while one was open for 7% of the time, Pallas kernels for 0%

profile of v2, /device:TPU:24, one launch (start us, length us, event | category | flops | bytes accessed | tf_op | source)
XLA Modules:
  0.0 179.9 jit_solution(9902598146999016107)
XLA Ops:
  0.7 11.3 %conditional.2 = (f32[16,128]{1,0:T(8,128)S(1)}, f32[16,128]{0,1:T(8,128)}) conditional(s32[]{:T(128)} %convert_element_type.12, (f32[25,16,128]{2,1,0:T(8,128)}, f32[25,16,128]{2,1,0:T(8,128)}, f32[16,128]{1,0:T(8,128)}, f32[16,128]{1,0:T(8,128)}) %tuple.29, () %tuple.25), branch_computations={%region_0.1_spmd, %region_1.2_spmd} | conditional | flops 10636288 | bytes 7602248 | solution.py:237
  0.7 0.8 copy.168
  1.7 0.8 copy.167
  3.4 0.3 fusion.7
  3.8 0.3 fusion.19
  4.1 0.3 fusion.5
  4.5 0.3 fusion.13
  4.8 0.3 fusion.3
  5.2 0.3 fusion.11
  5.6 0.6 bitcast_add_fusion
  6.2 0.4 copy.166
  6.6 0.4 copy.165
  7.1 1.2 convolution_bitcast_fusion.2
  8.2 1.0 fusion
  9.4 1.2 convolution_bitcast_fusion
  10.6 1.2 fusion.2
  12.0 75.1 %all_to_all.15.green_ref = f32[16,24,16,128]{3,2,1,0:T(8,128)S(1)} all-to-all(f32[16,24,16,128]{3,2,1,0:T(8,128)} %bitcast.194), channel_id=1, replica_groups=mesh['mom'=16,'hist'=16] {'mom'}, dimensions={0} | all-to-all | bytes 6291456 | tf_op jit(solution)/shard_map/all_to_all | solution.py:239
  87.2 5.4 %sigma.1 = f32[16,16,24,128]{3,2,1,0:T(8,128)S(1)} custom-call(bf16[2,256,256]{2,1,0:T(8,128)(2,1)S(1)} %copy-done.4, bf16[2,256,128]{2,1,0:T(8,128)(2,1)S(1)} %copy-done.6, bf16[2,256,256]{2,1,0:T(8,128)(2,1)S(1)} %copy-done.5, bf16[2,256,128]{2,1,0:T(8,128)(2,1)S(1)} %copy-done.7, f32[16,24,16,128]{3,2,1,0:T(8,128)S(1)} %all_to_all.15.green_ref, ...), custom_call_target="tpu_custom_call" | custom-call | flops 1610612736 | bytes 9437184 | tf_op jit(solution)/shard_map/sigma/pallas_call | solution.py:113
  92.5 1.6 copy-done
  94.2 9.3 %all-to-all-start.1 = ((f32[16,16,24,128]{3,2,1,0:T(8,128)}), f32[16,16,24,128]{3,2,1,0:T(8,128)S(1)}, u32[]{:S(2)}, u32[]{:S(2)}) async-start(f32[16,16,24,128]{3,2,1,0:T(8,128)} %copy-done), calls=%async_computation.1 | async-start | bytes 6291456 | tf_op jit(solution)/shard_map/all_to_all | solution.py:35
  104.2 2.7 %broadcast_select_fusion = f32[384,16,128]{2,1,0:T(8,128)S(1)} fusion(f32[384,16,128]{2,1,0:T(8,128)} %param.19, pred[384]{0:T(512)(128)(4,1)S(1)} %iota_compare_fusion), kind=kLoop, calls=%fused_computation.83 | loop fusion | flops 786432 | bytes 6291840 | tf_op jit(solution)/shard_map/jit(_where)/select_n | solution.py:243
  106.9 2.0 %copy.163 = f32[4,2,2,24,16,128]{5,4,3,2,1,0:T(8,128)} copy(f32[4,2,2,24,16,128]{5,4,3,2,0,1:T(8,128)S(1)} %bitcast.182) | data formatting | bytes 6291456 | tf_op jit(solution)/shard_map/transpose | solution.py:30
  108.9 3.6 %copy.164 = f32[384,16,128]{0,2,1:T(8,128)} copy(f32[384,16,128]{2,1,0:T(8,128)} %bitcast.183) | data formatting | bytes 6291456 | tf_op jit(solution)/shard_map/reshape;reshape | solution.py:244
  112.5 4.2 %fusion.54 = (bf16[16,128,384]{2,1,0:T(8,128)(2,1)}, bf16[16,128,384]{2,1,0:T(8,128)(2,1)}) fusion(f32[384,16,128]{0,2,1:T(8,128)} %copy.164), kind=kLoop, calls=%fused_computation.82 | loop fusion | flops 3145728 | bytes 6291456 | tf_op jit(solution)/shard_map/convert_element_type | solution.py:247
  116.8 0.7 conditional.3
  116.8 0.7 copy.182
  117.4 41.7 %all-to-all-done.1.sigma_ref = f32[16,16,24,128]{3,2,1,0:T(8,128)S(1)} async-done(((f32[16,16,24,128]{3,2,1,0:T(8,128)}), f32[16,16,24,128]{3,2,1,0:T(8,128)S(1)}, u32[]{:S(2)}, u32[]{:S(2)}) %all-to-all-start.1) | async-done | bytes 3145760 | tf_op jit(solution)/shard_map/all_to_all | solution.py:35
  159.2 1.4 copy-done.1
  160.6 1.4 copy-done.2
  162.0 1.7 history.1
  163.7 14.6 %all_to_all.16.parts_ref = f32[16,16,128]{2,1,0:T(8,128)} all-to-all(f32[16,16,128]{2,1,0:T(8,128)S(1)} %history.1), channel_id=1, replica_groups=mesh['mom'=16,'hist'=16] {'hist'}, dimensions={0} | all-to-all | bytes 262144 | tf_op jit(solution)/shard_map/all_to_all | solution.py:251
  178.2 1.7 finish.1
  (50 shorter events, 2.1 us)
Async XLA Ops:
  0.7 5.5 %copy-start.13 = (f32[25,16,128]{2,1,0:T(8,128)S(1)}, f32[25,16,128]{2,1,0:T(8,128)}, u32[]{:S(2)}) copy-start(f32[25,16,128]{2,1,0:T(8,128)} %get-tuple-element.77) | copy-start | bytes 614404 | tf_op jit(solution)/shard_map/cond
  0.7 5.9 %copy-start.12 = (f32[25,16,128]{2,1,0:T(8,128)S(1)}, f32[25,16,128]{2,1,0:T(8,128)}, u32[]{:S(2)}) copy-start(f32[25,16,128]{2,1,0:T(8,128)} %get-tuple-element.76) | copy-start | bytes 614404 | tf_op jit(solution)/shard_map/cond
  12.0 75.2 %copy-start.3 = (f32[24,256,128]{2,1,0:T(8,128)S(1)}, f32[24,256,128]{2,1,0:T(8,128)}, u32[]{:S(2)}) copy-start(f32[24,256,128]{2,1,0:T(8,128)} %screen_ref.1) | copy-start | bytes 9437188
  12.0 75.2 %copy-start.4 = (bf16[2,256,256]{2,1,0:T(8,128)(2,1)S(1)}, bf16[2,256,256]{2,1,0:T(8,128)(2,1)}, u32[]{:S(2)}) copy-start(bf16[2,256,256]{2,1,0:T(8,128)(2,1)} %constant.63.clone.to_space_ref) | copy-start | bytes 786436
  12.0 75.2 %copy-start.5 = (bf16[2,256,256]{2,1,0:T(8,128)(2,1)S(1)}, bf16[2,256,256]{2,1,0:T(8,128)(2,1)}, u32[]{:S(2)}) copy-start(bf16[2,256,256]{2,1,0:T(8,128)(2,1)} %constant.65.clone.back_ref) | copy-start | bytes 786436
  12.0 75.1 %copy-start.6 = (bf16[2,256,128]{2,1,0:T(8,128)(2,1)S(1)}, bf16[2,256,128]{2,1,0:T(8,128)(2,1)}, u32[]{:S(2)}) copy-start(bf16[2,256,128]{2,1,0:T(8,128)(2,1)} %constant.64.clone.to_space_low_ref) | copy-start | bytes 393220
  12.0 75.1 %copy-start.7 = (bf16[2,256,128]{2,1,0:T(8,128)(2,1)S(1)}, bf16[2,256,128]{2,1,0:T(8,128)(2,1)}, u32[]{:S(2)}) copy-start(bf16[2,256,128]{2,1,0:T(8,128)(2,1)} %constant.66.clone.back_low_ref) | copy-start | bytes 393220
  92.5 1.6 copy-start
  94.2 65.0 %all-to-all-start.1 = ((f32[16,16,24,128]{3,2,1,0:T(8,128)}), f32[16,16,24,128]{3,2,1,0:T(8,128)S(1)}, u32[]{:S(2)}, u32[]{:S(2)}) async-start(f32[16,16,24,128]{3,2,1,0:T(8,128)} %copy-done), calls=%async_computation.1 | async-start | bytes 6291456 | tf_op jit(solution)/shard_map/all_to_all | solution.py:35
  108.9 3.6 %copy-start.14 = (f32[16,128]{0,1:T(8,128)S(1)}, f32[16,128]{0,1:T(8,128)}, u32[]{:S(2)}) copy-start(f32[16,128]{0,1:T(8,128)} %get-tuple-element.116) | copy-start | bytes 24580
  108.9 3.6 %copy-start.15 = (f32[16,128]{1,0:T(8,128)S(1)}, f32[16,128]{1,0:T(8,128)}, u32[]{:S(2)}) copy-start(f32[16,128]{1,0:T(8,128)} %param.25) | copy-start | bytes 24580
  108.9 3.6 %copy-start.16 = (f32[16,128]{1,0:T(8,128)S(1)}, f32[16,128]{1,0:T(8,128)}, u32[]{:S(2)}) copy-start(f32[16,128]{1,0:T(8,128)} %param.24) | copy-start | bytes 24580
  116.8 42.4 %copy-start.8 = (bf16[128,128]{1,0:T(8,128)(2,1)S(1)}, bf16[128,128]{1,0:T(8,128)(2,1)}, u32[]{:S(2)}) copy-start(bf16[128,128]{1,0:T(8,128)(2,1)} %constant.67.clone.spread_ref) | copy-start | bytes 98308
  159.2 1.4 copy-start.1
  160.6 1.4 copy-start.2

commit v3 on v2

--- a/solution.py
+++ b/solution.py
@@ -22,12 +22,12 @@
 
 
 def exchange_order():
-    return np.arange(LAT).reshape(2, 4, 2).swapaxes(0, 1).reshape(LAT)
+    return np.arange(LAT).reshape(2, 8).swapaxes(0, 1).reshape(LAT)
 
 
 def ordered(blocks):
     rest = blocks.shape[1:]
-    return blocks.reshape(2, 4, 2, *rest).swapaxes(0, 1).reshape(LAT, *rest)
+    return blocks.reshape(2, 8, *rest).swapaxes(0, 1).reshape(LAT, *rest)
 
 
 def exchange(blocks):

time: 182 us -> 181 us (level)
  no operation moved by 1% of the time
where the time goes in v3:
time: 181 us; the launch traced here: 179 us
  blocking collectives  89.7 us (50%)
  waiting for transfers between devices  40.9 us (23%)
  local copies, waits for them, and re-layouts  14.6 us (8%)
  starting transfers between devices  9.33 us (5%)
  Pallas kernels  8.71 us (5%)
  other arithmetic  7.67 us (4%)
  matrix products  6.55 us (4%)
    all_to_all x1, blocking collectives, per_device(): lax.all_to_all(green_row.reshape(owners, own, local_k, ROW), 'mom', 0, 0)  75.1 us
    all_to_all x1, waiting for transfers between devices, exchange(): return lax.all_to_all(blocks, 'mom', 0, 0, axis_index_groups=groups)  40.9 us
    all_to_all x1, blocking collectives, per_device(): parts = lax.all_to_all(partial_sums, 'hist', 0, 0)  14.6 us
    all_to_all x1, starting transfers between devices, exchange(): return lax.all_to_all(blocks, 'mom', 0, 0, axis_index_groups=groups)  9.33 us
    pallas_call x1, Pallas kernels, sigma_of(): pl.pallas_call(sigma_kernel, out_shape=jax.ShapeDtypeStruct((LAT, LAT, sl...  5.37 us
    dot_general x4, matrix products, contract(): jnp.einsum('skab,skbc->kac', first, second, precision=HIGHEST)  4.52 us
    unnamed x24, local copies, waits for them, and re-layouts  4.5 us
    convert_element_type x1, other arithmetic, per_device(): (column - high).astype(jnp.bfloat16)  4.23 us
  transfers between devices with their start and end apart: 1, of which 1 were waited for; matrix products, arithmetic and copies ran while one was open for 7% of the time, Pallas kernels for 0%

profile of v3, /device:TPU:24, one launch (start us, length us, event | category | flops | bytes accessed | tf_op | source)
XLA Modules:
  0.0 179.0 jit_solution(15812023867201792726)
XLA Ops:
  0.7 11.3 %conditional.2 = (f32[16,128]{1,0:T(8,128)S(1)}, f32[16,128]{0,1:T(8,128)}) conditional(s32[]{:T(128)} %convert_element_type.12, (f32[25,16,128]{2,1,0:T(8,128)}, f32[25,16,128]{2,1,0:T(8,128)}, f32[16,128]{1,0:T(8,128)}, f32[16,128]{1,0:T(8,128)}) %tuple.29, () %tuple.25), branch_computations={%region_0.1_spmd, %region_1.2_spmd} | conditional | flops 10636288 | bytes 7602248 | solution.py:237
  0.7 0.8 copy.168
  1.7 0.8 copy.167
  3.4 0.3 fusion.7
  3.8 0.3 fusion.19
  4.1 0.3 fusion.5
  4.5 0.3 fusion.13
  4.8 0.3 fusion.3
  5.2 0.3 fusion.11
  5.6 0.6 bitcast_add_fusion
  6.2 0.4 copy.166
  6.6 0.4 copy.165
  7.1 1.2 convolution_bitcast_fusion.2
  8.2 1.0 fusion
  9.4 1.2 convolution_bitcast_fusion
  10.6 1.2 fusion.2
  12.0 75.1 %all_to_all.15.green_ref = f32[16,24,16,128]{3,2,1,0:T(8,128)S(1)} all-to-all(f32[16,24,16,128]{3,2,1,0:T(8,128)} %bitcast.194), channel_id=1, replica_groups=mesh['mom'=16,'hist'=16] {'mom'}, dimensions={0} | all-to-all | bytes 6291456 | tf_op jit(solution)/shard_map/all_to_all | solution.py:239
  87.2 5.4 %sigma.1 = f32[16,16,24,128]{3,2,1,0:T(8,128)S(1)} custom-call(bf16[2,256,256]{2,1,0:T(8,128)(2,1)S(1)} %copy-done.4, bf16[2,256,128]{2,1,0:T(8,128)(2,1)S(1)} %copy-done.6, bf16[2,256,256]{2,1,0:T(8,128)(2,1)S(1)} %copy-done.5, bf16[2,256,128]{2,1,0:T(8,128)(2,1)S(1)} %copy-done.7, f32[16,24,16,128]{3,2,1,0:T(8,128)S(1)} %all_to_all.15.green_ref, ...), custom_call_target="tpu_custom_call" | custom-call | flops 1610612736 | bytes 9437184 | tf_op jit(solution)/shard_map/sigma/pallas_call | solution.py:113
  92.5 1.6 copy-done
  94.2 9.3 %all-to-all-start.1 = ((f32[16,16,24,128]{3,2,1,0:T(8,128)}), f32[16,16,24,128]{3,2,1,0:T(8,128)S(1)}, u32[]{:S(2)}, u32[]{:S(2)}) async-start(f32[16,16,24,128]{3,2,1,0:T(8,128)} %copy-done), calls=%async_computation.1 | async-start | bytes 6291456 | tf_op jit(solution)/shard_map/all_to_all | solution.py:35
  104.2 2.7 %broadcast_select_fusion = f32[384,16,128]{2,1,0:T(8,128)S(1)} fusion(f32[384,16,128]{2,1,0:T(8,128)} %param.19, pred[384]{0:T(512)(128)(4,1)S(1)} %iota_compare_fusion), kind=kLoop, calls=%fused_computation.83 | loop fusion | flops 786432 | bytes 6291840 | tf_op jit(solution)/shard_map/jit(_where)/select_n | solution.py:243
  106.9 2.0 %copy.163 = f32[8,2,24,16,128]{4,3,2,1,0:T(8,128)} copy(f32[8,2,24,16,128]{4,3,2,0,1:T(8,128)S(1)} %bitcast.182) | data formatting | bytes 6291456 | tf_op jit(solution)/shard_map/transpose | solution.py:30
  108.9 3.6 %copy.164 = f32[384,16,128]{0,2,1:T(8,128)} copy(f32[384,16,128]{2,1,0:T(8,128)} %bitcast.183) | data formatting | bytes 6291456 | tf_op jit(solution)/shard_map/reshape;reshape | solution.py:244
  112.5 4.2 %fusion.54 = (bf16[16,128,384]{2,1,0:T(8,128)(2,1)}, bf16[16,128,384]{2,1,0:T(8,128)(2,1)}) fusion(f32[384,16,128]{0,2,1:T(8,128)} %copy.164), kind=kLoop, calls=%fused_computation.82 | loop fusion | flops 3145728 | bytes 6291456 | tf_op jit(solution)/shard_map/convert_element_type | solution.py:247
  116.8 0.7 conditional.3
  116.8 0.7 copy.182
  117.4 40.9 %all-to-all-done.1.sigma_ref = f32[16,16,24,128]{3,2,1,0:T(8,128)S(1)} async-done(((f32[16,16,24,128]{3,2,1,0:T(8,128)}), f32[16,16,24,128]{3,2,1,0:T(8,128)S(1)}, u32[]{:S(2)}, u32[]{:S(2)}) %all-to-all-start.1) | async-done | bytes 3145760 | tf_op jit(solution)/shard_map/all_to_all | solution.py:35
  158.3 1.4 copy-done.1
  159.7 1.4 copy-done.2
  161.1 1.7 history.1
  162.8 14.6 %all_to_all.16.parts_ref = f32[16,16,128]{2,1,0:T(8,128)} all-to-all(f32[16,16,128]{2,1,0:T(8,128)S(1)} %history.1), channel_id=1, replica_groups=mesh['mom'=16,'hist'=16] {'hist'}, dimensions={0} | all-to-all | bytes 262144 | tf_op jit(solution)/shard_map/all_to_all | solution.py:251
  177.3 1.7 finish.1
  (50 shorter events, 2.1 us)
Async XLA Ops:
  0.7 5.5 %copy-start.13 = (f32[25,16,128]{2,1,0:T(8,128)S(1)}, f32[25,16,128]{2,1,0:T(8,128)}, u32[]{:S(2)}) copy-start(f32[25,16,128]{2,1,0:T(8,128)} %get-tuple-element.77) | copy-start | bytes 614404 | tf_op jit(solution)/shard_map/cond
  0.7 5.9 %copy-start.12 = (f32[25,16,128]{2,1,0:T(8,128)S(1)}, f32[25,16,128]{2,1,0:T(8,128)}, u32[]{:S(2)}) copy-start(f32[25,16,128]{2,1,0:T(8,128)} %get-tuple-element.76) | copy-start | bytes 614404 | tf_op jit(solution)/shard_map/cond
  12.0 75.2 %copy-start.3 = (f32[24,256,128]{2,1,0:T(8,128)S(1)}, f32[24,256,128]{2,1,0:T(8,128)}, u32[]{:S(2)}) copy-start(f32[24,256,128]{2,1,0:T(8,128)} %screen_ref.1) | copy-start | bytes 9437188
  12.0 75.2 %copy-start.4 = (bf16[2,256,256]{2,1,0:T(8,128)(2,1)S(1)}, bf16[2,256,256]{2,1,0:T(8,128)(2,1)}, u32[]{:S(2)}) copy-start(bf16[2,256,256]{2,1,0:T(8,128)(2,1)} %constant.63.clone.to_space_ref) | copy-start | bytes 786436
  12.0 75.2 %copy-start.5 = (bf16[2,256,256]{2,1,0:T(8,128)(2,1)S(1)}, bf16[2,256,256]{2,1,0:T(8,128)(2,1)}, u32[]{:S(2)}) copy-start(bf16[2,256,256]{2,1,0:T(8,128)(2,1)} %constant.65.clone.back_ref) | copy-start | bytes 786436
  12.0 75.1 %copy-start.6 = (bf16[2,256,128]{2,1,0:T(8,128)(2,1)S(1)}, bf16[2,256,128]{2,1,0:T(8,128)(2,1)}, u32[]{:S(2)}) copy-start(bf16[2,256,128]{2,1,0:T(8,128)(2,1)} %constant.64.clone.to_space_low_ref) | copy-start | bytes 393220
  12.0 75.1 %copy-start.7 = (bf16[2,256,128]{2,1,0:T(8,128)(2,1)S(1)}, bf16[2,256,128]{2,1,0:T(8,128)(2,1)}, u32[]{:S(2)}) copy-start(bf16[2,256,128]{2,1,0:T(8,128)(2,1)} %constant.66.clone.back_low_ref) | copy-start | bytes 393220
  92.5 1.6 copy-start
  94.2 64.1 %all-to-all-start.1 = ((f32[16,16,24,128]{3,2,1,0:T(8,128)}), f32[16,16,24,128]{3,2,1,0:T(8,128)S(1)}, u32[]{:S(2)}, u32[]{:S(2)}) async-start(f32[16,16,24,128]{3,2,1,0:T(8,128)} %copy-done), calls=%async_computation.1 | async-start | bytes 6291456 | tf_op jit(solution)/shard_map/all_to_all | solution.py:35
  108.9 3.6 %copy-start.14 = (f32[16,128]{0,1:T(8,128)S(1)}, f32[16,128]{0,1:T(8,128)}, u32[]{:S(2)}) copy-start(f32[16,128]{0,1:T(8,128)} %get-tuple-element.116) | copy-start | bytes 24580
  108.9 3.6 %copy-start.15 = (f32[16,128]{1,0:T(8,128)S(1)}, f32[16,128]{1,0:T(8,128)}, u32[]{:S(2)}) copy-start(f32[16,128]{1,0:T(8,128)} %param.25) | copy-start | bytes 24580
  108.9 3.6 %copy-start.16 = (f32[16,128]{1,0:T(8,128)S(1)}, f32[16,128]{1,0:T(8,128)}, u32[]{:S(2)}) copy-start(f32[16,128]{1,0:T(8,128)} %param.24) | copy-start | bytes 24580
  116.8 41.5 %copy-start.8 = (bf16[128,128]{1,0:T(8,128)(2,1)S(1)}, bf16[128,128]{1,0:T(8,128)(2,1)}, u32[]{:S(2)}) copy-start(bf16[128,128]{1,0:T(8,128)(2,1)} %constant.67.clone.spread_ref) | copy-start | bytes 98308
  158.3 1.4 copy-start.1
  159.7 1.4 copy-start.2
